TPU v7x, 128 devices: a whole 4x4x4 slice. The times are simulated.
128 devices in a mesh: owner: 8 (over x, core), fsdp: 16 (over y, z).
Axes of the slice: x: 4, y: 4, z: 4, core: 2. Of those that a mesh axis runs over, the one named last changes fastest.
Arguments:
- precond: bfloat16 [8, 2048, 2048], P('owner', 'fsdp'), as said below
- basis_old: bfloat16 [8, 2048, 2048], P('owner', 'fsdp'), as said below
- gradient: bfloat16 [16384, 8192], P('owner', 'fsdp'), may hold values from -6 to 6
- moment_in: float32 [16384, 8192], P('owner', 'fsdp')
- second_in: float32 [16384, 8192], P('owner', 'fsdp'), may hold values from 0.3 to 3
Outputs:
- update: bfloat16 [16384, 8192], P('owner', 'fsdp')
- moment_one: float32 [16384, 8192], P('owner', 'fsdp')
- moment_two: float32 [16384, 8192], P('owner', 'fsdp')
- basis_new: float32 [8, 2048, 2048], P('owner', 'fsdp')
Inputs may be any that keep to these rules, and one draw needn't show every extreme that they name: Each block of precond is symmetric and positive definite. Each block of basis_old is invertible.
All inputs are finite; a program needn't handle non-finite values.
Results may differ from a plain program's by a relative error of at most 0.024.
Values may be sent and summed in bfloat16 or wider, within the bound.
No kernel may reach another device: no remote copies, remote signals or barrier semaphores. Data moves between devices by JAX's collectives and lax.ppermute only.
A program may use at most 192 MiB of HBM per device.

v0:
```python
import jax
import jax.numpy as jnp
from jax import lax
from jax.sharding import PartitionSpec as P

beta_one = 0.9
beta_two = 0.95
small_eps = 1e-08
norm_eps = 1e-06


def pack_gram(full, half):
    top = full[:, :half, half:]
    mixed = jnp.triu(full[:, :half, :half]) + jnp.tril(full[:, half:, half:], -1)
    diagonal = jnp.diagonal(full[:, half:, half:], axis1=1, axis2=2)
    return (jnp.stack([top, mixed], axis=1), diagonal)


def unpack_gram(packed, diagonal, half):
    top = packed[:, 0]
    mixed = packed[:, 1]
    corner = jnp.triu(mixed) + jnp.swapaxes(jnp.triu(mixed, 1), 1, 2)
    strict = jnp.tril(mixed, -1)
    lower = (
        strict
        + jnp.swapaxes(strict, 1, 2)
        + diagonal[:, :, None] * jnp.eye(half, dtype=jnp.float32)[None]
    )
    upper_band = jnp.concatenate([corner, top], axis=2)
    lower_band = jnp.concatenate([jnp.swapaxes(top, 1, 2), lower], axis=2)
    return jnp.concatenate([upper_band, lower_band], axis=1)


def orthonormal(chol, power):

    def solve_one(factor, rows):
        return jax.scipy.linalg.solve_triangular(factor, rows.T, lower=True).T

    return jax.vmap(solve_one)(chol, power)


def on_device(precond, basis_old, gradient, moment_in, second_in):
    blocks = precond.shape[0]
    order = precond.shape[2]
    half = order // 2
    width = gradient.shape[1]
    power = jnp.einsum(
        "bik,bkj->bij",
        precond,
        lax.all_gather(basis_old, "fsdp", axis=1, tiled=True),
        preferred_element_type=jnp.float32,
    )
    power_half = power.astype(jnp.bfloat16)
    partial_gram = jnp.einsum(
        "bki,bkj->bij", power_half, power_half, preferred_element_type=jnp.float32
    )
    packed, diagonal = pack_gram(partial_gram, half)
    packed_sum, diagonal_sum = lax.psum((packed, diagonal), "fsdp")
    gram_sum = unpack_gram(packed_sum, diagonal_sum, half)
    chol = jnp.linalg.cholesky(gram_sum)
    basis_new = orthonormal(chol, power_half.astype(jnp.float32))
    basis_half = basis_new.astype(jnp.bfloat16)
    moment_one = beta_one * moment_in + (1.0 - beta_one) * gradient.astype(jnp.float32)
    moment_half = moment_one.astype(jnp.bfloat16)
    gradient_block_list = gradient.reshape(blocks, order, width)
    moment_block_list = moment_half.reshape(blocks, order, width)
    complete_basis = lax.all_gather(basis_half, "fsdp", axis=1, tiled=True)
    rotated_gradient = jnp.einsum(
        "aos,aol->asl", complete_basis, gradient_block_list, preferred_element_type=jnp.float32
    )
    rotated_moment = jnp.einsum(
        "aos,aol->asl", complete_basis, moment_block_list, preferred_element_type=jnp.float32
    )
    moment_two = beta_two * second_in.reshape(blocks, order, width) + (1.0 - beta_two) * jnp.square(
        rotated_gradient
    )
    step_ratio = (rotated_moment / (jnp.sqrt(moment_two) + small_eps)).astype(jnp.bfloat16)
    unscaled_update = jnp.einsum(
        "rfu,rup->rfp", complete_basis, step_ratio, preferred_element_type=jnp.float32
    )
    total = lax.psum(jnp.sum(unscaled_update * unscaled_update), ("owner", "fsdp"))
    count = gradient.shape[0] * lax.axis_size("owner") * width * lax.axis_size("fsdp")
    scale = jnp.sqrt(jnp.float32(count)) / (jnp.sqrt(total) + norm_eps)
    update = (unscaled_update * scale).reshape(blocks * order, width).astype(jnp.bfloat16)
    return (update, moment_one, moment_two.reshape(blocks * order, width), basis_new)


def solution(mesh):
    return jax.shard_map(
        on_device,
        mesh=mesh,
        in_specs=(
            P("owner", "fsdp", None),
            P("owner", "fsdp", None),
            P("owner", "fsdp"),
            P("owner", "fsdp"),
            P("owner", "fsdp"),
        ),
        out_specs=(
            P("owner", "fsdp"),
            P("owner", "fsdp"),
            P("owner", "fsdp"),
            P("owner", "fsdp", None),
        ),
        check_vma=False,
    )
```

profile of v0, /device:TPU:0, one launch (start us, length us, event | category | flops | bytes accessed | tf_op | source)
XLA Modules:
  0.0 1275.9 jit_solution(16252286923377315585)
XLA Ops:
  8.0 75.6 %all-gather.3.cloned.1.call-done = bf16[1,2048,2048]{2,1,0:T(8,128)(2,1)} async-done(((bf16[1,128,2048]{2,1,0:T(8,128)(2,1)}), bf16[1,2048,2048]{2,1,0:T(8,128)(2,1)}) %all-gather.3.cloned.1.call-update) | async-done | bytes 8388624 | tf_op jit(solution)/shard_map/all_gather | solution.py:50
  103.6 17.3 %gather_fusion = f32[1024]{0:T(1024)S(1)} fusion(f32[1024,1024]{1,0:T(8,128)} %get-tuple-element.30, s32[1024]{0:T(1024)S(1)} %bitcast.802), kind=kCustom, calls=%fused_computation | custom fusion | bytes 16384 | tf_op jit(solution)/shard_map/jit(diagonal)/gather | solution.py:15
  120.9 39.1 %psum.25 = f32[1024]{0:T(1024)S(1)} all-reduce(f32[1024]{0:T(1024)S(1)} %gather_fusion), channel_id=1, replica_groups=mesh['owner'=8,'fsdp'=16] {'fsdp'}, use_global_device_ids=true, to_apply=%region_1.2 | all-reduce | flops 1024 | bytes 8192 | tf_op jit(solution)/shard_map/psum | solution.py:58
  160.0 80.9 %all-reduce.3.cloned.1.call-done = f32[1,2,1024,1024]{3,2,1,0:T(8,128)} async-done(((f32[1,2,1024,1024]{3,2,1,0:T(8,128)}), f32[1,2,1024,1024]{3,2,1,0:T(8,128)}) %all-reduce.3.cloned.1.call-update) | async-done | bytes 8388624 | tf_op jit(solution)/shard_map/psum | solution.py:58
  308.1 17.6 %copy.42 = f32[1,2048,2048]{2,1,0:T(8,128)} copy(f32[1,2048,2048]{1,2,0:T(8,128)} %maximum_maximum_fusion) | data formatting | bytes 33554432 | tf_op jit(solution)/shard_map/concatenate | solution.py:31
  325.6 13.6 %fusion = f32[1,2048,2048]{2,1,0:T(8,128)S(1)} fusion(f32[1,2048,2048]{2,1,0:T(8,128)} %copy.42, f32[1,1024,1024]{1,2,0:T(8,128)} %copy-done.4, f32[1,1024,1024]{1,2,0:T(8,128)} %get-tuple-element.34, f32[1,1024,2048]{1,2,0:T(8,128)} %copy.41), kind=kLoop, calls=%fused_computation.6 | loop fusion | flops 16777216 | bytes 50331648 | tf_op jit(solution)/shard_map/jit(cholesky)/div | solution.py:60
  345.0 11.7 custom-call.143
  379.7 11.9 custom-call.145
  407.3 11.7 custom-call.147
  436.6 11.7 custom-call.149
  466.3 11.7 custom-call.151
  496.2 11.9 custom-call.153
  526.5 11.7 custom-call.155
  539.5 10.0 custom-call.156
  556.9 11.7 custom-call.157
  570.0 10.2 custom-call.158
  587.5 11.7 custom-call.159
  617.7 11.7 custom-call.161
  647.6 11.7 custom-call.163
  676.8 12.1 custom-call.165
  705.9 11.7 custom-call.167
  718.9 9.9 custom-call.168
  734.1 11.7 custom-call.169
  761.2 12.1 custom-call.171
  787.9 11.7 custom-call.173
  811.4 12.5 select_select_fusion
  823.9 56.1 %while.1 = (s32[]{:T(128)}, f32[1,2048,2048]{2,1,0:T(8,128)}, s32[16,2]{0,1:T(2,128)S(1)}, f32[16,1,128,128]{3,2,1,0:T(8,128)}, s32[]{:T(128)}) while((s32[]{:T(128)}, f32[1,2048,2048]{2,1,0:T(8,128)}, s32[16,2]{0,1:T(2,128)S(1)}, f32[16,1,128,128]{3,2,1,0:T(8,128)}, s32[]{:T(128)}) %tuple.177), condition=%wide.while_cond, body=%wide.while_body.sunk | while | flops 2 | bytes 132705 | solution.py:37
  880.0 158.8 %custom-call.174 = f32[1,16,128,128]{2,3,1,0:T(8,128)} custom-call(f32[1,16,128,128]{3,2,1,0:T(8,128)} %bitcast.810), custom_call_target="InvertDiagBlocksLowerTriangular" | custom-call | tf_op jit(solution)/shard_map/vmap(jit(_solve_triangular))/triangular_solve | solution.py:37
  1095.9 70.6 %all-gather.5.cloned.1.call-done = bf16[1,2048,2048]{1,2,0:T(8,128)(2,1)} async-done(((bf16[1,128,2048]{1,2,0:T(8,128)(2,1)}), bf16[1,2048,2048]{1,2,0:T(8,128)(2,1)}) %all-gather.5.cloned.1.call-update) | async-done | bytes 8388624 | tf_op jit(solution)/shard_map/all_gather | solution.py:67
  1166.5 12.0 multiply_add_fusion
  1178.5 21.1 %multiply_reduce_fusion = (f32[]{:T(128)}, f32[2048,512]{1,0:T(8,128)}) fusion(f32[2048,512]{1,0:T(8,128)} %multiply_add_fusion, bf16[1,2048,2048]{1,2,0:T(8,128)(2,1)} %all-gather.5.cloned.1.call-done, f32[2048,512]{1,0:T(8,128)} %multiply_add_fusion.1), kind=kOutput, calls=%fused_computation.29 | convolution fusion | flops 8596226048 | bytes 20971524 | tf_op jit(solution)/shard_map/rfu,rup->rfp/dot_general | solution.py:78
  1199.6 64.5 %psum.26 = f32[]{:T(128)} all-reduce(f32[]{:T(128)} %get-tuple-element.215), channel_id=1, replica_groups=mesh['owner'=8,'fsdp'=16] {'owner','fsdp'}, use_global_device_ids=true, to_apply=%region_35.36 | all-reduce | flops 1 | bytes 8 | tf_op jit(solution)/shard_map/psum | solution.py:81
  (209 shorter events, 448.4 us)
Async XLA Ops:
  7.2 76.4 %copy-start = (bf16[1,128,2048]{2,1,0:T(8,128)(2,1)S(1)}, bf16[1,128,2048]{2,1,0:T(8,128)(2,1)}, u32[]{:S(2)}) copy-start(bf16[1,128,2048]{2,1,0:T(8,128)(2,1)} %param.5) | copy-start | bytes 1572868
  7.2 76.3 %all-gather.3.cloned.1.call-start = ((), (), s32[]{:S(2)}) async-start(), calls=%async_computation | async-start | bytes 8912896 | tf_op jit(solution)/shard_map/all_gather | solution.py:50
  7.9 233.0 %all-reduce.3.cloned.1.call-start = ((), (), s32[]{:S(2)}) async-start(), calls=%async_computation.1 | async-start | bytes 16777216 | tf_op jit(solution)/shard_map/psum | solution.py:58
  98.8 1067.6 %all-gather.5.cloned.1.call-start = ((), (), s32[]{:S(2)}) async-start(), calls=%async_computation.2 | async-start | bytes 8912896 | tf_op jit(solution)/shard_map/all_gather | solution.py:67
  291.2 7.0 copy-start.2
  296.2 2.0 copy-start.4
  339.2 5.7 copy-start.3
  1178.5 90.5 %copy-start.1 = (bf16[1,128,2048]{2,1,0:T(8,128)(2,1)S(1)}, bf16[1,128,2048]{2,1,0:T(8,128)(2,1)}, u32[]{:S(2)}) copy-start(bf16[1,128,2048]{2,1,0:T(8,128)(2,1)} %param.5) | copy-start | bytes 1572868
Sparse Core Ops, SparseCore 0:
  10.2 73.3 all-gather.2
  99.0 141.9 all-reduce.2
  1089.1 77.2 all-gather.4
where the time goes:
time: 1290 us; the launch traced here: 1280 us
  other arithmetic  591 us (46%)
  waiting for transfers between devices  228 us (18%)
  matrix products  183 us (14%)
  local copies, waits for them, and re-layouts  146 us (11%)
  blocking collectives  104 us (8%)
  between operations  25.4 us (2%)
    another operation x62, other arithmetic, on_device(): chol = jnp.linalg.cholesky(gram_sum)  356 us
    another operation x3, other arithmetic, solve_one(): return jax.scipy.linalg.solve_triangular(factor, rows.T, lower=True).T  171 us
    another operation x30, matrix products, on_device(): chol = jnp.linalg.cholesky(gram_sum)  92.5 us
    psum x1, waiting for transfers between devices, on_device(): packed_sum, diagonal_sum = lax.psum((packed, diagonal), 'fsdp')  80.9 us
    all_gather x1, waiting for transfers between devices, on_device(): lax.all_gather(basis_old, 'fsdp', axis=1, tiled=True)  75.6 us
    all_gather x1, waiting for transfers between devices, on_device(): complete_basis = lax.all_gather(basis_half, 'fsdp', axis=1, tiled=True)  70.6 us
    psum x1, blocking collectives, on_device(): lax.psum(jnp.sum(unscaled_update * unscaled_update), ('owner', 'fsdp'))  64.5 us
    another operation x48, local copies, waits for them, and re-layouts  56 us
  transfers between devices with their start and end apart: 3, of which 3 were waited for; matrix products, arithmetic and copies ran while one was open for 2% of the time, Pallas kernels for 0%

commit v1 on v0

v1 whole, which is shorter than its diff:
```python
import functools
import jax
import jax.numpy as jnp
from jax import lax
from jax.experimental import pallas as pl
from jax.experimental.pallas import tpu as pltpu
from jax.sharding import PartitionSpec as P

beta_one = 0.9
beta_two = 0.95
small_eps = 1e-08
norm_eps = 1e-06
NN = (((1,), (0,)), ((), ()))
NT = (((1,), (1,)), ((), ()))
TN = (((0,), (0,)), ((), ()))
CH = 256
FIRST = 512

def lane_splat(row, lane):
    return jnp.broadcast_to(row[:, lane:lane+1], (8, 128))

def diag_pick(row, start):
    idx = lax.broadcasted_iota(jnp.int32, (8, 128), 0) + start
    return jnp.take_along_axis(row, idx, axis=1, mode="promise_in_bounds")

def invert_factor(A):
    sub = lax.broadcasted_iota(jnp.int32, (8, 128), 0)
    lane = lax.broadcasted_iota(jnp.int32, (8, 128), 1)
    A = list(A)
    X = [(lane == sub + 8 * g).astype(jnp.float32) for g in range(16)]
    for g in range(16):
        r = [jnp.broadcast_to(A[g][k:k+1, :], (8, 128)) for k in range(8)]
        x = [jnp.broadcast_to(X[g][k:k+1, :], (8, 128)) for k in range(8)]
        d = {}
        for j in range(8):
            for i in range(j, 8):
                d[i, j] = lane_splat(r[j], 8 * g + i)
        for k in range(8):
            rs = lax.rsqrt(d[k, k])
            rd = rs * rs
            for i in range(k + 1, 8):
                m = d[i, k] * rd
                for j in range(k + 1, i + 1):
                    d[i, j] = d[i, j] - m * d[j, k]
                r[i] = r[i] - m * r[k]
                x[i] = x[i] - m * x[k]
            r[k] = r[k] * rs
            x[k] = x[k] * rs
        for h in range(g + 1, 16):
            for k in range(8):
                l = diag_pick(r[k], 8 * h)
                A[h] = A[h] - l * r[k]
                X[h] = X[h] - l * x[k]
        z = x[0]
        for k in range(1, 8):
            z = jnp.where(sub == k, x[k], z)
        X[g] = z
    return X


def mm(a, b, dims=NN):
    return lax.dot_general(a, b, dims, preferred_element_type=jnp.float32)

def split(x):
    high = x.astype(jnp.bfloat16)
    return high, (x - high.astype(jnp.float32)).astype(jnp.bfloat16)

def mm3(a, b, dims=NN):
    ah, al = split(a)
    bh, bl = split(b)
    return mm(ah, bh, dims) + (mm(al, bh, dims) + mm(ah, bl, dims))

def inverse_of_rows(block):
    rows = invert_factor([block[8 * i:8 * i + 8, :] for i in range(16)])
    return jnp.concatenate(rows, axis=0)

def kernel(prev, count, *refs):
    if prev:
        t_ref, ph_ref, pl_ref, rh, rl, v = refs
        rh[0:prev, :] = ph_ref[...]
        rl[0:prev, :] = pl_ref[...]
    else:
        t_ref, rh, rl, v = refs

    def chunk(ci, carry):
        row = pl.multiple_of(ci * CH, CH)
        out = pl.multiple_of(prev + ci * CH, CH)
        t = t_ref[pl.ds(row, CH), :]
        v[...] = t.astype(jnp.float32)

        def remove(p, carry):
            at = pl.ds(pl.multiple_of(p * CH, CH), CH)
            qh = rh[at, :]
            ql = rl[at, :]
            t = t_ref[pl.ds(row, CH), :]
            s = mm(t, qh, NT) + mm(t, ql, NT)
            sh, sl = split(s)
            v[...] -= mm(sh, qh) + (mm(sl, qh) + mm(sh, ql))
            return carry

        lax.fori_loop(0, prev // CH + ci, remove, 0)
        vh, vl = split(v[...])
        g = mm(vh, vh, NT) + (mm(vh, vl, NT) + mm(vl, vh, NT))
        h = CH // 2
        x1 = inverse_of_rows(g[:h, :h])
        u = mm3(x1, g[:h, h:])
        ut = u.T
        s = g[h:, h:] - mm3(ut, u)
        w = mm3(ut, x1)
        x2 = inverse_of_rows(s)
        x21 = -mm3(x2, w)
        x = jnp.concatenate([jnp.concatenate([x1, jnp.zeros((h, h), jnp.float32)], axis=1),
                             jnp.concatenate([x21, x2], axis=1)], axis=0)
        xh, xl = split(x)
        vh, vl = split(v[...])
        q = mm(xh, vh) + (mm(xl, vh) + mm(xh, vl))
        qh, ql = split(q)
        rh[pl.ds(out, CH), :] = qh
        rl[pl.ds(out, CH), :] = ql
        return carry

    lax.fori_loop(0, count // CH, chunk, 0)

def orthogonal_rows(t, done=None):
    count, width = t.shape
    prev = 0 if done is None else done[0].shape[0]
    shape = jax.ShapeDtypeStruct((prev + count, width), jnp.bfloat16)
    args = (t,) if done is None else (t,) + tuple(done)
    n = prev + count
    return pl.pallas_call(
        functools.partial(kernel, prev, count),
        out_shape=(shape, shape),
        scratch_shapes=[pltpu.VMEM((CH, width), jnp.float32)],
        compiler_params=pltpu.CompilerParams(vmem_limit_bytes=56 * 1024 * 1024),
    )(*args)


def sum_over_all(x):
    for axis in ("owner", "fsdp"):
        size = lax.axis_size(axis)
        step = 1
        while step < size:
            x = x + lax.ppermute(x, axis, [(i, i ^ step) for i in range(size)])
            step *= 2
    return x


def on_device(precond, basis_old, gradient, moment_in, second_in):
    order = precond.shape[2]
    width = gradient.shape[1]
    both = jnp.concatenate([precond[0], basis_old[0, :, :FIRST]], axis=1)
    both = lax.all_gather(both, "fsdp", axis=0, tiled=True)
    factor = both[:, :order]
    later = lax.all_gather(basis_old[0, :, FIRST:], "fsdp", axis=0, tiled=True)
    moment_one = beta_one * moment_in + (1.0 - beta_one) * gradient.astype(jnp.float32)
    moment_half = moment_one.astype(jnp.bfloat16)
    first_rows = mm(both[:, order:], factor, TN).astype(jnp.bfloat16)
    first = orthogonal_rows(first_rows)
    later_rows = mm(later, factor, TN).astype(jnp.bfloat16)
    high, low = orthogonal_rows(later_rows, first)
    part = order // lax.axis_size("fsdp")
    start = lax.axis_index("fsdp") * part
    basis_new = (
        lax.dynamic_slice_in_dim(high, start, part, 1).astype(jnp.float32)
        + lax.dynamic_slice_in_dim(low, start, part, 1).astype(jnp.float32)
    ).T[None]
    rotated_gradient = mm(high, gradient)
    rotated_moment = mm(high, moment_half)
    moment_two = beta_two * second_in + (1.0 - beta_two) * jnp.square(rotated_gradient)
    step_ratio = (rotated_moment / (jnp.sqrt(moment_two) + small_eps)).astype(jnp.bfloat16)
    unscaled_update = mm(high, step_ratio, TN)
    total = sum_over_all(jnp.sum(unscaled_update * unscaled_update).reshape(1, 1))
    count = gradient.shape[0] * lax.axis_size("owner") * width * lax.axis_size("fsdp")
    scale = jnp.sqrt(jnp.float32(count)) / (jnp.sqrt(total) + norm_eps)
    update = (unscaled_update * scale).astype(jnp.bfloat16)
    return (update, moment_one, moment_two, basis_new)


def solution(mesh):
    return jax.shard_map(
        on_device,
        mesh=mesh,
        in_specs=(
            P("owner", "fsdp", None),
            P("owner", "fsdp", None),
            P("owner", "fsdp"),
            P("owner", "fsdp"),
            P("owner", "fsdp"),
        ),
        out_specs=(
            P("owner", "fsdp"),
            P("owner", "fsdp"),
            P("owner", "fsdp"),
            P("owner", "fsdp", None),
        ),
        check_vma=False,
    )
```

time: 1290 us -> 416 us (0.32)
  other arithmetic: 591 us -> 12.2 us
  Pallas kernels: 0 us -> 188 us
  local copies, waits for them, and re-layouts: 146 us -> 4.13 us
  waiting for transfers between devices: 228 us -> 105 us
  matrix products: 183 us -> 60.9 us
  blocking collectives: 104 us -> 0 us
  starting transfers between devices: 0.12 us -> 21.5 us
    another operation x66 -> x0, other arithmetic: 531 us -> none  [the longest x62 356 us: on_device(): chol = jnp.linalg.cholesky(gram_sum)]
    pallas_call x0 -> x2, Pallas kernels: none -> 188 us  [orthogonal_rows(): pl.pallas_call(functools.partial(kernel, prev, count), out_shape=(shape,...]
    another operation x61 -> x0, matrix products: 142 us -> none  [the longest x30 92.5 us: on_device(): chol = jnp.linalg.cholesky(gram_sum)]
    psum x2 -> x0, blocking collectives: 104 us -> none  [the longest x1 64.5 us: on_device(): lax.psum(jnp.sum(unscaled_update * unscaled_update), ('owner', 'fsdp'))]
    psum x1 -> x0, waiting for transfers between devices: 80.9 us -> none  [on_device(): packed_sum, diagonal_sum = lax.psum((packed, diagonal), 'fsdp')]
    another operation x65 -> x0, local copies, waits for them, and re-layouts: 64 us -> none
    all_gather x2, waiting for transfers between devices: 146 us -> 99 us  [the longest x1 76.8 us: on_device(): both = lax.all_gather(both, 'fsdp', axis=0, tiled=True)]
    concatenate x2 -> x0, local copies, waits for them, and re-layouts: 26.8 us -> none  [the longest x1 17.6 us: unpack_gram(): return jnp.concatenate([upper_band, lower_band], axis=1)]
  transfers between devices with their start and end apart: 3 -> 9, of which waited for: 3 -> 9; matrix products, arithmetic and copies ran while one was open for 2% -> 4% of each run, Pallas kernels for 0% -> 8%
where the time goes in v1:
time: 416 us; the launch traced here: 412 us
  Pallas kernels  188 us (45%)
  waiting for transfers between devices  105 us (25%)
  matrix products  60.9 us (15%)
  starting transfers between devices  21.5 us (5%)
  between operations  19.5 us (5%)
  other arithmetic  12.2 us (3%)
    pallas_call x2, Pallas kernels, orthogonal_rows(): pl.pallas_call(functools.partial(kernel, prev, count), out_shape=(shape,...  188 us
    all_gather x1, waiting for transfers between devices, on_device(): both = lax.all_gather(both, 'fsdp', axis=0, tiled=True)  76.8 us
    dot_general x4, matrix products, mm(): return lax.dot_general(a, b, dims, preferred_element_type=jnp.float32)  60.9 us
    all_gather x1, waiting for transfers between devices, on_device(): later = lax.all_gather(basis_old[0, :, FIRST:], 'fsdp', axis=0, tiled=True)  22.2 us
    ppermute x7, starting transfers between devices, sum_over_all(): x = x + lax.ppermute(x, axis, [(i, i ^ step) for i in range(size)])  21.4 us
  transfers between devices with their start and end apart: 9, of which 9 were waited for; matrix products, arithmetic and copies ran while one was open for 4% of the time, Pallas kernels for 8%

profile of v1, /device:TPU:0, one launch (start us, length us, event | category | flops | bytes accessed | tf_op | source)
XLA Modules:
  0.0 411.6 jit_solution(4303092555559952185)
XLA Ops:
  7.2 0.0 all-gather.4.cloned.1.call-start
  7.2 1.1 slice_bitcast_fusion
  8.3 1.9 pad_maximum_fusion
  10.2 0.0 all-gather.4.cloned.1.call-update
  10.2 0.0 all-gather.6.cloned.1.call-start
  10.3 1.8 slice.14
  12.1 4.9 %multiply_add_fusion.1 = f32[2048,512]{1,0:T(8,128)} fusion(bf16[2048,512]{1,0:T(8,128)(2,1)S(1)} %copy-done, f32[2048,512]{1,0:T(8,128)} %param.8), kind=kLoop, calls=%fused_computation.10 | loop fusion | flops 4194304 | bytes 10485760 | tf_op jit(solution)/shard_map/add | solution.py:155
  17.0 76.8 %all-gather.4.cloned.1.call-done = bf16[2048,2560]{1,0:T(8,128)(2,1)} async-done(((bf16[128,2560]{1,0:T(8,128)(2,1)}), bf16[2048,2560]{1,0:T(8,128)(2,1)}) %all-gather.4.cloned.1.call-update) | async-done | bytes 10485776 | tf_op jit(solution)/shard_map/all_gather | solution.py:152
  93.8 9.9 %fusion.7.refs_0_ = bf16[512,2048]{1,0:T(8,128)(2,1)} fusion(bf16[2048,2560]{1,0:T(8,128)(2,1)} %all-gather.4.cloned.1.call-done), kind=kOutput, calls=%fused_computation.11 | convolution fusion | flops 4296015872 | bytes 12582912 | tf_op jit(solution)/shard_map/dot_general | solution.py:62
  103.7 31.1 %shard_map.84 = (bf16[512,2048]{1,0:T(8,128)(2,1)}, bf16[512,2048]{1,0:T(8,128)(2,1)}) custom-call(bf16[512,2048]{1,0:T(8,128)(2,1)} %fusion.7.refs_0_), custom_call_target="tpu_custom_call" | custom-call | tf_op jit(solution)/shard_map/pallas_call | solution.py:130
  134.9 22.2 %all-gather.6.cloned.1.call-done = bf16[1,2048,1536]{2,1,0:T(8,128)(2,1)} async-done(((bf16[1,128,1536]{2,1,0:T(8,128)(2,1)}), bf16[1,2048,1536]{2,1,0:T(8,128)(2,1)}) %all-gather.6.cloned.1.call-update) | async-done | bytes 6291472 | tf_op jit(solution)/shard_map/all_gather | solution.py:154
  157.1 19.6 %fusion.3.refs_0_ = bf16[1536,2048]{1,0:T(8,128)(2,1)} fusion(bf16[2048,2560]{1,0:T(8,128)(2,1)} %all-gather.4.cloned.1.call-done, bf16[1,2048,1536]{2,1,0:T(8,128)(2,1)} %all-gather.6.cloned.1.call-done), kind=kOutput, calls=%fused_computation.4 | convolution fusion | flops 12888047616 | bytes 20971520 | tf_op jit(solution)/shard_map/dot_general | solution.py:62
  176.7 157.2 %shard_map.85 = (bf16[2048,2048]{1,0:T(8,128)(2,1)}, bf16[2048,2048]{1,0:T(8,128)(2,1)}) custom-call(bf16[1536,2048]{1,0:T(8,128)(2,1)} %fusion.3.refs_0_, bf16[512,2048]{1,0:T(8,128)(2,1)} %get-tuple-element.8.refs_1_, bf16[512,2048]{1,0:T(8,128)(2,1)} %get-tuple-element.9.refs_2_), custom_call_target="tpu_custom_call" | custom-call | tf_op jit(solution)/shard_map/pallas_call | solution.py:130
  333.9 1.3 add_bitcast_fusion
  335.2 1.3 copy.10
  336.5 10.6 %multiply_add_fusion = f32[2048,512]{1,0:T(8,128)} fusion(f32[2048,512]{1,0:T(8,128)} %param.9, bf16[2048,2048]{1,0:T(8,128)(2,1)} %get-tuple-element.10, bf16[2048,512]{1,0:T(8,128)(2,1)S(1)} %copy-done), kind=kOutput, calls=%fused_computation.9 | convolution fusion | flops 4299161600 | bytes 18874368 | tf_op jit(solution)/shard_map/dot_general | solution.py:62
  347.1 20.8 %multiply_reduce_fusion = (f32[]{:T(128)}, f32[2048,512]{1,0:T(8,128)}) fusion(bf16[2048,2048]{1,0:T(8,128)(2,1)} %get-tuple-element.10, f32[2048,512]{1,0:T(8,128)} %multiply_add_fusion, f32[2048,512]{1,0:T(8,128)} %multiply_add_fusion.1), kind=kOutput, calls=%fused_computation.7 | convolution fusion | flops 8596226048 | bytes 20971524 | tf_op jit(solution)/shard_map/dot_general | solution.py:62
  367.9 0.2 collective-permute-start
  368.1 1.2 collective-permute-done
  370.6 2.8 collective-permute-start.1
  373.4 0.8 collective-permute-done.1
  374.8 4.3 %collective-permute-start.2 = (f32[1,1]{1,0:T(1,128)}, f32[1,1]{1,0:T(1,128)}, u32[]{:S(2)}, u32[]{:S(2)}) collective-permute-start(f32[1,1]{1,0:T(1,128)} %add.48), channel_id=1, source_target_pairs={{0,64},{16,80},{32,96},{48,112},{64,0},{80,16},{96,32},{112,48},{1... | collective-permute-start | bytes 20 | tf_op jit(solution)/shard_map/ppermute | solution.py:143
  379.1 0.8 collective-permute-done.2
  380.5 2.6 collective-permute-start.3
  383.2 0.9 collective-permute-done.3
  384.7 4.3 %collective-permute-start.4 = (f32[1,1]{1,0:T(1,128)}, f32[1,1]{1,0:T(1,128)}, u32[]{:S(2)}, u32[]{:S(2)}) collective-permute-start(f32[1,1]{1,0:T(1,128)} %add.50), channel_id=1, source_target_pairs={{0,2},{1,3},{2,0},{3,1},{4,6},{5,7},{6,4},{7,5},{8,10},{9,11},{10,... | collective-permute-start | bytes 20 | tf_op jit(solution)/shard_map/ppermute | solution.py:143
  389.1 0.8 collective-permute-done.4
  390.4 2.8 collective-permute-start.5
  393.3 0.8 collective-permute-done.5
  394.6 4.3 %collective-permute-start.6 = (f32[1,1]{1,0:T(1,128)}, f32[1,1]{1,0:T(1,128)}, u32[]{:S(2)}, u32[]{:S(2)}) collective-permute-start(f32[1,1]{1,0:T(1,128)} %add.52), channel_id=1, source_target_pairs={{0,8},{1,9},{2,10},{3,11},{4,12},{5,13},{6,14},{7,15},{8,0},{9,1},... | collective-permute-start | bytes 20 | tf_op jit(solution)/shard_map/ppermute | solution.py:143
  399.0 0.8 collective-permute-done.6
  400.4 4.1 multiply_convert_fusion
  (3 shorter events, 0.0 us)
Async XLA Ops:
  7.2 4.9 %copy-start = (bf16[2048,512]{1,0:T(8,128)(2,1)S(1)}, bf16[2048,512]{1,0:T(8,128)(2,1)}, u32[]{:S(2)}) copy-start(bf16[2048,512]{1,0:T(8,128)(2,1)} %param.7) | copy-start | bytes 6291460
  7.2 86.6 %all-gather.4.cloned.1.call-start = ((), (), s32[]{:S(2)}) async-start(), calls=%async_computation | async-start | bytes 11141120 | tf_op jit(solution)/shard_map/all_gather | solution.py:152
  10.2 146.9 %all-gather.6.cloned.1.call-start = ((), (), s32[]{:S(2)}) async-start(), calls=%async_computation.1 | async-start | bytes 6684672 | tf_op jit(solution)/shard_map/all_gather | solution.py:154
  367.9 1.4 collective-permute-start
  370.6 3.6 collective-permute-start.1
  374.8 5.1 %collective-permute-start.2 = (f32[1,1]{1,0:T(1,128)}, f32[1,1]{1,0:T(1,128)}, u32[]{:S(2)}, u32[]{:S(2)}) collective-permute-start(f32[1,1]{1,0:T(1,128)} %add.48), channel_id=1, source_target_pairs={{0,64},{16,80},{32,96},{48,112},{64,0},{80,16},{96,32},{112,48},{1... | collective-permute-start | bytes 20 | tf_op jit(solution)/shard_map/ppermute | solution.py:143
  380.5 3.6 collective-permute-start.3
  384.7 5.1 %collective-permute-start.4 = (f32[1,1]{1,0:T(1,128)}, f32[1,1]{1,0:T(1,128)}, u32[]{:S(2)}, u32[]{:S(2)}) collective-permute-start(f32[1,1]{1,0:T(1,128)} %add.50), channel_id=1, source_target_pairs={{0,2},{1,3},{2,0},{3,1},{4,6},{5,7},{6,4},{7,5},{8,10},{9,11},{10,... | collective-permute-start | bytes 20 | tf_op jit(solution)/shard_map/ppermute | solution.py:143
  390.4 3.6 collective-permute-start.5
  394.6 5.1 %collective-permute-start.6 = (f32[1,1]{1,0:T(1,128)}, f32[1,1]{1,0:T(1,128)}, u32[]{:S(2)}, u32[]{:S(2)}) collective-permute-start(f32[1,1]{1,0:T(1,128)} %add.52), channel_id=1, source_target_pairs={{0,8},{1,9},{2,10},{3,11},{4,12},{5,13},{6,14},{7,15},{8,0},{9,1},... | collective-permute-start | bytes 20 | tf_op jit(solution)/shard_map/ppermute | solution.py:143
Sparse Core Ops, SparseCore 0:
  10.8 82.9 all-gather.3
  96.0 61.0 all-gather.5

commit v2 on v1

--- a/solution.py
+++ b/solution.py
@@ -14,7 +14,7 @@
 NT = (((1,), (1,)), ((), ()))
 TN = (((0,), (0,)), ((), ()))
 CH = 256
-FIRST = 512
+FIRST = 768
 
 def lane_splat(row, lane):
     return jnp.broadcast_to(row[:, lane:lane+1], (8, 128))
@@ -74,52 +74,80 @@
     rows = invert_factor([block[8 * i:8 * i + 8, :] for i in range(16)])
     return jnp.concatenate(rows, axis=0)
 
+def inverse_of_chunk(g):
+    h = CH // 2
+    x1 = inverse_of_rows(g[:h, :h])
+    u = mm3(x1, g[:h, h:])
+    ut = u.T
+    w = mm3(ut, x1)
+    x2 = inverse_of_rows(g[h:, h:] - mm3(ut, u))
+    x21 = -mm3(x2, w)
+    top = jnp.concatenate([x1, jnp.zeros((h, h), jnp.float32)], axis=1)
+    return jnp.concatenate([top, jnp.concatenate([x21, x2], axis=1)], axis=0)
+
 def kernel(prev, count, *refs):
     if prev:
-        t_ref, ph_ref, pl_ref, rh, rl, v = refs
+        t_ref, ph_ref, pl_ref, rh, rl, v, vh, vl, sh, sl = refs
         rh[0:prev, :] = ph_ref[...]
         rl[0:prev, :] = pl_ref[...]
     else:
-        t_ref, rh, rl, v = refs
-
-    def chunk(ci, carry):
-        row = pl.multiple_of(ci * CH, CH)
-        out = pl.multiple_of(prev + ci * CH, CH)
-        t = t_ref[pl.ds(row, CH), :]
-        v[...] = t.astype(jnp.float32)
-
-        def remove(p, carry):
-            at = pl.ds(pl.multiple_of(p * CH, CH), CH)
-            qh = rh[at, :]
-            ql = rl[at, :]
-            t = t_ref[pl.ds(row, CH), :]
-            s = mm(t, qh, NT) + mm(t, ql, NT)
-            sh, sl = split(s)
-            v[...] -= mm(sh, qh) + (mm(sl, qh) + mm(sh, ql))
-            return carry
-
-        lax.fori_loop(0, prev // CH + ci, remove, 0)
-        vh, vl = split(v[...])
-        g = mm(vh, vh, NT) + (mm(vh, vl, NT) + mm(vl, vh, NT))
-        h = CH // 2
-        x1 = inverse_of_rows(g[:h, :h])
-        u = mm3(x1, g[:h, h:])
-        ut = u.T
-        s = g[h:, h:] - mm3(ut, u)
-        w = mm3(ut, x1)
-        x2 = inverse_of_rows(s)
-        x21 = -mm3(x2, w)
-        x = jnp.concatenate([jnp.concatenate([x1, jnp.zeros((h, h), jnp.float32)], axis=1),
-                             jnp.concatenate([x21, x2], axis=1)], axis=0)
+        t_ref, rh, rl, v, vh, vl, sh, sl = refs
+    width = t_ref.shape[1]
+    tiles = [slice(a, a + CH) for a in range(0, width, CH)]
+    chunks = count // CH
+
+    def remove(c, depth):
+        slot = c % 2
+        t = t_ref[c * CH:(c + 1) * CH, :]
+        for p in range(0, depth, CH):
+            at = slice(p, p + CH)
+            sh[:, at], sl[:, at] = split(mm(t, rh[at, :], NT) + mm(t, rl[at, :], NT))
+        for a in tiles:
+            x = t_ref[c * CH:(c + 1) * CH, a].astype(jnp.float32)
+            if depth:
+                x = x - (mm(sh[:, :depth], rh[:depth, a]) + (mm(sl[:, :depth], rh[:depth, a]) + mm(sh[:, :depth], rl[:depth, a])))
+            v[slot, :, a] = x
+            vh[slot, :, a], vl[slot, :, a] = split(x)
+
+    def products(c, d):
+        a, b = c % 2, d % 2
+        low = mm(vh[a], vl[b], NT)
+        other = low.T if c == d else mm(vl[a], vh[b], NT)
+        return mm(vh[a], vh[b], NT) + (low + other)
+
+    def finish(c, x):
+        slot = c % 2
         xh, xl = split(x)
-        vh, vl = split(v[...])
-        q = mm(xh, vh) + (mm(xl, vh) + mm(xh, vl))
-        qh, ql = split(q)
-        rh[pl.ds(out, CH), :] = qh
-        rl[pl.ds(out, CH), :] = ql
-        return carry
-
-    lax.fori_loop(0, count // CH, chunk, 0)
+        at = slice(prev + c * CH, prev + (c + 1) * CH)
+        for a in tiles:
+            q = mm(xh, vh[slot, :, a]) + (mm(xl, vh[slot, :, a]) + mm(xh, vl[slot, :, a]))
+            rh[at, a], rl[at, a] = split(q)
+
+    def correct(c, s):
+        slot = c % 2
+        th, tl = split(s.T)
+        at = slice(prev + (c - 1) * CH, prev + c * CH)
+        for a in tiles:
+            x = v[slot, :, a] - (mm(th, rh[at, a]) + (mm(tl, rh[at, a]) + mm(th, rl[at, a])))
+            v[slot, :, a] = x
+            vh[slot, :, a], vl[slot, :, a] = split(x)
+
+    remove(0, prev)
+    g = products(0, 0)
+    x = s = None
+    for c in range(chunks):
+        if c:
+            finish(c - 1, x)
+            correct(c, s)
+        if c + 1 < chunks:
+            remove(c + 1, prev + c * CH)
+            cross = products(c, c + 1)
+            ahead = products(c + 1, c + 1)
+        x = inverse_of_chunk(g)
+        if c + 1 < chunks:
+            s = mm3(x, cross)
+            g = ahead - mm3(s.T, s)
+    finish(chunks - 1, x)
 
 def orthogonal_rows(t, done=None):
     count, width = t.shape
@@ -130,19 +158,17 @@
     return pl.pallas_call(
         functools.partial(kernel, prev, count),
         out_shape=(shape, shape),
-        scratch_shapes=[pltpu.VMEM((CH, width), jnp.float32)],
+        scratch_shapes=[pltpu.VMEM((2, CH, width), jnp.float32)] + [pltpu.VMEM((2, CH, width), jnp.bfloat16)] * 2
+        + [pltpu.VMEM((CH, n), jnp.bfloat16)] * 2,
         compiler_params=pltpu.CompilerParams(vmem_limit_bytes=56 * 1024 * 1024),
     )(*args)
 
 
 def sum_over_all(x):
-    for axis in ("owner", "fsdp"):
-        size = lax.axis_size(axis)
-        step = 1
-        while step < size:
-            x = x + lax.ppermute(x, axis, [(i, i ^ step) for i in range(size)])
-            step *= 2
-    return x
+    axes = ("owner", "fsdp")
+    size = lax.axis_size(axes)
+    copies = jnp.broadcast_to(x, (size, 128))
+    return jnp.sum(lax.all_to_all(copies, axes, 0, 0, tiled=True)[:, :1], axis=0, keepdims=True)
 
 
 def on_device(precond, basis_old, gradient, moment_in, second_in):

time: 416 us -> 326 us (0.78)
  Pallas kernels: 188 us -> 120 us
  starting transfers between devices: 21.5 us -> 8.33 us
  waiting for transfers between devices: 105 us -> 99.9 us
  between operations: 19.5 us -> 15 us
    pallas_call x2, Pallas kernels: 188 us -> 120 us  [orthogonal_rows(): pl.pallas_call(functools.partial(kernel, prev, count), out_shape=(shape,...]
    ppermute x7 -> x0, starting transfers between devices: 21.4 us -> none  [sum_over_all(): x = x + lax.ppermute(x, axis, [(i, i ^ step) for i in range(size)])]
    all_gather x1, waiting for transfers between devices: 22.2 us -> 11.5 us  [on_device(): later = lax.all_gather(basis_old[0, :, FIRST:], 'fsdp', axis=0, tiled=True)]
    all_to_all x0 -> x1, starting transfers between devices: none -> 8.25 us  [sum_over_all(): lax.all_to_all(copies, axes, 0, 0, tiled=True)[:, :1]]
    all_to_all x0 -> x1, waiting for transfers between devices: none -> 6.77 us  [sum_over_all(): lax.all_to_all(copies, axes, 0, 0, tiled=True)[:, :1]]
    ppermute x7 -> x0, waiting for transfers between devices: 5.98 us -> none  [sum_over_all(): x = x + lax.ppermute(x, axis, [(i, i ^ step) for i in range(size)])]
    all_gather x1, waiting for transfers between devices: 76.8 us -> 81.6 us  [on_device(): both = lax.all_gather(both, 'fsdp', axis=0, tiled=True)]
  transfers between devices with their start and end apart: 9 -> 3, of which waited for: 9 -> 3; matrix products, arithmetic and copies ran while one was open for 4% -> 7% of each run, Pallas kernels for 8% -> 11%
where the time goes in v2:
time: 326 us; the launch traced here: 321 us
  Pallas kernels  120 us (37%)
  waiting for transfers between devices  99.9 us (31%)
  matrix products  59.7 us (18%)
  between operations  15 us (5%)
  other arithmetic  12.9 us (4%)
  starting transfers between devices  8.33 us (3%)
  local copies, waits for them, and re-layouts  5.43 us (2%)
    pallas_call x2, Pallas kernels, orthogonal_rows(): pl.pallas_call(functools.partial(kernel, prev, count), out_shape=(shape,...  120 us
    all_gather x1, waiting for transfers between devices, on_device(): both = lax.all_gather(both, 'fsdp', axis=0, tiled=True)  81.6 us
    dot_general x4, matrix products, mm(): return lax.dot_general(a, b, dims, preferred_element_type=jnp.float32)  59.7 us
    all_gather x1, waiting for transfers between devices, on_device(): later = lax.all_gather(basis_old[0, :, FIRST:], 'fsdp', axis=0, tiled=True)  11.5 us
    all_to_all x1, starting transfers between devices, sum_over_all(): lax.all_to_all(copies, axes, 0, 0, tiled=True)[:, :1]  8.25 us
    all_to_all x1, waiting for transfers between devices, sum_over_all(): lax.all_to_all(copies, axes, 0, 0, tiled=True)[:, :1]  6.77 us
  transfers between devices with their start and end apart: 3, of which 3 were waited for; matrix products, arithmetic and copies ran while one was open for 7% of the time, Pallas kernels for 11%

profile of v2, /device:TPU:0, one launch (start us, length us, event | category | flops | bytes accessed | tf_op | source)
XLA Modules:
  0.0 321.3 jit_solution(13414862206012662793)
XLA Ops:
  7.2 0.0 copy-start
  7.2 0.0 all-gather.4.cloned.1.call-start
  7.2 1.1 slice_bitcast_fusion
  8.3 2.0 pad_maximum_fusion
  10.3 0.0 all-gather.4.cloned.1.call-update
  10.3 0.0 all-gather.6.cloned.1.call-start
  10.3 1.7 slice.17
  12.1 0.0 all-gather.6.cloned.1.call-update
  12.1 0.0 copy-done
  12.1 4.9 %multiply_add_fusion.1 = f32[2048,512]{1,0:T(8,128)} fusion(bf16[2048,512]{1,0:T(8,128)(2,1)S(1)} %copy-done, f32[2048,512]{1,0:T(8,128)} %param.8), kind=kLoop, calls=%fused_computation.10 | loop fusion | flops 4194304 | bytes 10485760 | tf_op jit(solution)/shard_map/add | solution.py:181
  17.0 81.6 %all-gather.4.cloned.1.call-done = bf16[2048,2816]{1,0:T(8,128)(2,1)} async-done(((bf16[128,2816]{1,0:T(8,128)(2,1)}), bf16[2048,2816]{1,0:T(8,128)(2,1)}) %all-gather.4.cloned.1.call-update) | async-done | bytes 11534352 | tf_op jit(solution)/shard_map/all_gather | solution.py:178
  98.6 12.2 %fusion.7.refs_0_ = bf16[768,2048]{1,0:T(8,128)(2,1)} fusion(bf16[2048,2816]{1,0:T(8,128)(2,1)} %all-gather.4.cloned.1.call-done), kind=kOutput, calls=%fused_computation.11 | convolution fusion | flops 6444023808 | bytes 14680064 | tf_op jit(solution)/shard_map/dot_general | solution.py:62
  110.8 35.2 %shard_map.84 = (bf16[768,2048]{1,0:T(8,128)(2,1)}, bf16[768,2048]{1,0:T(8,128)(2,1)}) custom-call(bf16[768,2048]{1,0:T(8,128)(2,1)} %fusion.7.refs_0_), custom_call_target="tpu_custom_call" | custom-call | tf_op jit(solution)/shard_map/pallas_call | solution.py:158
  146.0 11.5 %all-gather.6.cloned.1.call-done = bf16[1,2048,1280]{2,1,0:T(8,128)(2,1)} async-done(((bf16[1,128,1280]{2,1,0:T(8,128)(2,1)}), bf16[1,2048,1280]{2,1,0:T(8,128)(2,1)}) %all-gather.6.cloned.1.call-update) | async-done | bytes 5242896 | tf_op jit(solution)/shard_map/all_gather | solution.py:180
  157.5 16.8 %fusion.3.refs_0_ = bf16[1280,2048]{1,0:T(8,128)(2,1)} fusion(bf16[2048,2816]{1,0:T(8,128)(2,1)} %all-gather.4.cloned.1.call-done, bf16[1,2048,1280]{2,1,0:T(8,128)(2,1)} %all-gather.6.cloned.1.call-done), kind=kOutput, calls=%fused_computation.4 | convolution fusion | flops 10740039680 | bytes 18874368 | tf_op jit(solution)/shard_map/dot_general | solution.py:62
  174.3 0.0 copy-start.1
  174.3 84.7 %shard_map.85 = (bf16[2048,2048]{1,0:T(8,128)(2,1)}, bf16[2048,2048]{1,0:T(8,128)(2,1)}) custom-call(bf16[1280,2048]{1,0:T(8,128)(2,1)} %fusion.3.refs_0_, bf16[768,2048]{1,0:T(8,128)(2,1)} %get-tuple-element.8.refs_1_, bf16[768,2048]{1,0:T(8,128)(2,1)} %get-tuple-element.9.refs_2_), custom_call_target="tpu_custom_call" | custom-call | tf_op jit(solution)/shard_map/pallas_call | solution.py:158
  259.0 0.0 copy-done.1
  259.0 10.1 %multiply_add_fusion = f32[2048,512]{1,0:T(8,128)} fusion(f32[2048,512]{1,0:T(8,128)S(1)} %copy-done.1, bf16[2048,2048]{1,0:T(8,128)(2,1)} %get-tuple-element.10, bf16[2048,512]{1,0:T(8,128)(2,1)S(1)} %copy-done), kind=kOutput, calls=%fused_computation.9 | convolution fusion | flops 4299161600 | bytes 18874368 | tf_op jit(solution)/shard_map/dot_general | solution.py:62
  269.1 20.8 %multiply_reduce_fusion = (f32[]{:T(128)}, f32[2048,512]{1,0:T(8,128)}) fusion(bf16[2048,2048]{1,0:T(8,128)(2,1)} %get-tuple-element.10, f32[2048,512]{1,0:T(8,128)} %multiply_add_fusion, f32[2048,512]{1,0:T(8,128)} %multiply_add_fusion.1), kind=kOutput, calls=%fused_computation.7 | convolution fusion | flops 8596226048 | bytes 20971524 | tf_op jit(solution)/shard_map/dot_general | solution.py:62
  289.8 1.3 broadcast_in_dim.4
  291.1 8.3 %all-to-all-start = ((f32[128,1,128]{2,1,0:T(1,128)}), f32[128,1,128]{2,1,0:T(1,128)S(1)}, u32[]{:S(2)}, u32[]{:S(2)}) async-start(f32[128,1,128]{2,1,0:T(1,128)} %broadcast_in_dim.4), calls=%async_computation | async-start | bytes 131072 | tf_op jit(solution)/shard_map/all_to_all | solution.py:171
  299.4 1.3 add_bitcast_fusion
  300.7 1.3 copy.15
  302.0 6.8 %all-to-all-done = f32[128,1,128]{2,1,0:T(1,128)S(1)} async-done(((f32[128,1,128]{2,1,0:T(1,128)}), f32[128,1,128]{2,1,0:T(1,128)S(1)}, u32[]{:S(2)}, u32[]{:S(2)}) %all-to-all-start) | async-done | bytes 65568 | tf_op jit(solution)/shard_map/all_to_all | solution.py:171
  308.8 0.6 slice_reduce_fusion
  310.1 4.1 %multiply_convert_fusion = bf16[2048,512]{1,0:T(8,128)(2,1)} fusion(f32[2048,512]{1,0:T(8,128)} %get-tuple-element.25, f32[]{:T(128)S(6)} %div.8), kind=kLoop, calls=%fused_computation.6 | loop fusion | flops 2097152 | bytes 6291460 | tf_op jit(solution)/shard_map/convert_element_type | solution.py:201
Async XLA Ops:
  7.2 4.9 %copy-start = (bf16[2048,512]{1,0:T(8,128)(2,1)S(1)}, bf16[2048,512]{1,0:T(8,128)(2,1)}, u32[]{:S(2)}) copy-start(bf16[2048,512]{1,0:T(8,128)(2,1)} %param.7) | copy-start | bytes 6291460
  7.2 91.5 %all-gather.4.cloned.1.call-start = ((), (), s32[]{:S(2)}) async-start(), calls=%async_computation.1 | async-start | bytes 12255232 | tf_op jit(solution)/shard_map/all_gather | solution.py:178
  10.3 147.2 %all-gather.6.cloned.1.call-start = ((), (), s32[]{:S(2)}) async-start(), calls=%async_computation.2 | async-start | bytes 5570560 | tf_op jit(solution)/shard_map/all_gather | solution.py:180
  174.3 84.7 %copy-start.1 = (f32[2048,512]{1,0:T(8,128)S(1)}, f32[2048,512]{1,0:T(8,128)}, u32[]{:S(2)}) copy-start(f32[2048,512]{1,0:T(8,128)} %param.9) | copy-start | bytes 12582916
  291.1 17.7 %all-to-all-start = ((f32[128,1,128]{2,1,0:T(1,128)}), f32[128,1,128]{2,1,0:T(1,128)S(1)}, u32[]{:S(2)}, u32[]{:S(2)}) async-start(f32[128,1,128]{2,1,0:T(1,128)} %broadcast_in_dim.4), calls=%async_computation | async-start | bytes 131072 | tf_op jit(solution)/shard_map/all_to_all | solution.py:171
Sparse Core Ops, SparseCore 0:
  10.8 87.8 all-gather.3
  101.4 56.0 all-gather.5

commit v3 on v2

--- a/solution.py
+++ b/solution.py
@@ -14,7 +14,8 @@
 NT = (((1,), (1,)), ((), ()))
 TN = (((0,), (0,)), ((), ()))
 CH = 256
-FIRST = 768
+FIRST = 1024
+BAND = 512
 
 def lane_splat(row, lane):
     return jnp.broadcast_to(row[:, lane:lane+1], (8, 128))
@@ -87,7 +88,7 @@
 
 def kernel(prev, count, *refs):
     if prev:
-        t_ref, ph_ref, pl_ref, rh, rl, v, vh, vl, sh, sl = refs
+        t_ref, ph_ref, pl_ref, rh, own, v, vh, vl, sh, sl, rl = refs
         rh[0:prev, :] = ph_ref[...]
         rl[0:prev, :] = pl_ref[...]
     else:
@@ -148,6 +149,10 @@
             s = mm3(x, cross)
             g = ahead - mm3(s.T, s)
     finish(chunks - 1, x)
+    if prev:
+        part = own.shape[1]
+        at = pl.ds(pl.multiple_of(lax.axis_index("fsdp") * part, part), part)
+        own[...] = rh[:, at].astype(jnp.float32) + rl[:, at].astype(jnp.float32)
 
 def orthogonal_rows(t, done=None):
     count, width = t.shape
@@ -155,13 +160,62 @@
     shape = jax.ShapeDtypeStruct((prev + count, width), jnp.bfloat16)
     args = (t,) if done is None else (t,) + tuple(done)
     n = prev + count
+    scratch = [pltpu.VMEM((2, CH, width), jnp.float32)] + [pltpu.VMEM((2, CH, width), jnp.bfloat16)] * 2
+    scratch += [pltpu.VMEM((CH, n), jnp.bfloat16)] * 2
+    outs = (shape, shape)
+    if prev:
+        scratch += [pltpu.VMEM((n, width), jnp.bfloat16)]
+        outs = (shape, jax.ShapeDtypeStruct((n, width // lax.axis_size("fsdp")), jnp.float32))
     return pl.pallas_call(
         functools.partial(kernel, prev, count),
-        out_shape=(shape, shape),
-        scratch_shapes=[pltpu.VMEM((2, CH, width), jnp.float32)] + [pltpu.VMEM((2, CH, width), jnp.bfloat16)] * 2
-        + [pltpu.VMEM((CH, n), jnp.bfloat16)] * 2,
+        out_shape=outs,
+        scratch_shapes=scratch,
         compiler_params=pltpu.CompilerParams(vmem_limit_bytes=56 * 1024 * 1024),
     )(*args)
+
+
+def rotate_kernel(q_ref, gradient_ref, moment_ref, second_ref, two_ref, raw_ref, square_ref):
+    step = pl.program_id(0)
+    q = q_ref[...]
+    order = q.shape[1]
+    width = gradient_ref.shape[1]
+
+    @pl.when(step == 0)
+    def _():
+        raw_ref[...] = jnp.zeros_like(raw_ref)
+
+    for a in range(0, width, CH):
+        at = slice(a, a + CH)
+        grad_rot = mm(q, gradient_ref[:, at])
+        moment_rot = mm(q, moment_ref[:, at])
+        two = beta_two * second_ref[:, at] + (1.0 - beta_two) * jnp.square(grad_rot)
+        two_ref[:, at] = two
+        ratio = (moment_rot / (jnp.sqrt(two) + small_eps)).T.astype(jnp.bfloat16)
+        for o in range(0, order, CH):
+            raw_ref[at, o:o + CH] += mm(ratio, q_ref[:, o:o + CH])
+
+    @pl.when(step == pl.num_programs(0) - 1)
+    def _():
+        square_ref[...] = jnp.sum(jnp.square(raw_ref[...]), axis=0, keepdims=True)
+
+
+def rotate(basis, gradient, moment_half, second_in):
+    rows, order = basis.shape
+    width = gradient.shape[1]
+    whole = pl.BlockSpec((order, width), lambda i: (0, 0))
+    band = pl.BlockSpec((BAND, width), lambda i: (i, 0))
+    return pl.pallas_call(
+        rotate_kernel,
+        grid=(rows // BAND,),
+        in_specs=[pl.BlockSpec((BAND, order), lambda i: (i, 0)), whole, whole, band],
+        out_specs=(band, pl.BlockSpec((width, order), lambda i: (0, 0)), pl.BlockSpec((1, order), lambda i: (0, 0))),
+        out_shape=(
+            jax.ShapeDtypeStruct((rows, width), jnp.float32),
+            jax.ShapeDtypeStruct((width, order), jnp.float32),
+            jax.ShapeDtypeStruct((1, order), jnp.float32),
+        ),
+        compiler_params=pltpu.CompilerParams(vmem_limit_bytes=48 * 1024 * 1024),
+    )(basis, gradient, moment_half, second_in)
 
 
 def sum_over_all(x):
@@ -183,19 +237,11 @@
     first_rows = mm(both[:, order:], factor, TN).astype(jnp.bfloat16)
     first = orthogonal_rows(first_rows)
     later_rows = mm(later, factor, TN).astype(jnp.bfloat16)
-    high, low = orthogonal_rows(later_rows, first)
-    part = order // lax.axis_size("fsdp")
-    start = lax.axis_index("fsdp") * part
-    basis_new = (
-        lax.dynamic_slice_in_dim(high, start, part, 1).astype(jnp.float32)
-        + lax.dynamic_slice_in_dim(low, start, part, 1).astype(jnp.float32)
-    ).T[None]
-    rotated_gradient = mm(high, gradient)
-    rotated_moment = mm(high, moment_half)
-    moment_two = beta_two * second_in + (1.0 - beta_two) * jnp.square(rotated_gradient)
-    step_ratio = (rotated_moment / (jnp.sqrt(moment_two) + small_eps)).astype(jnp.bfloat16)
-    unscaled_update = mm(high, step_ratio, TN)
-    total = sum_over_all(jnp.sum(unscaled_update * unscaled_update).reshape(1, 1))
+    high, own = orthogonal_rows(later_rows, first)
+    basis_new = own.T[None]
+    moment_two, turned, squares = rotate(high, gradient, moment_half, second_in)
+    unscaled_update = lax.optimization_barrier(turned.T)
+    total = sum_over_all(jnp.sum(squares).reshape(1, 1))
     count = gradient.shape[0] * lax.axis_size("owner") * width * lax.axis_size("fsdp")
     scale = jnp.sqrt(jnp.float32(count)) / (jnp.sqrt(total) + norm_eps)
     update = (unscaled_update * scale).astype(jnp.bfloat16)

time: 326 us -> 309 us (0.948)
  matrix products: 59.7 us -> 28.5 us
  Pallas kernels: 120 us -> 138 us
  waiting for transfers between devices: 99.9 us -> 95.1 us
    dot_general x4 -> x2, matrix products: 59.7 us -> 28.5 us  [mm(): return lax.dot_general(a, b, dims, preferred_element_type=jnp.float32)]
    pallas_call x2 -> x3, Pallas kernels: 120 us -> 138 us  [the longest x2 117 us: orthogonal_rows(): pl.pallas_call(functools.partial(kernel, prev, count), out_shape=outs, sc...]
    all_gather x1, waiting for transfers between devices: 11.5 us -> 0.01 us  [on_device(): later = lax.all_gather(basis_old[0, :, FIRST:], 'fsdp', axis=0, tiled=True)]
    convert_element_type x0 -> x1, other arithmetic: none -> 5.7 us  [on_device(): moment_half = moment_one.astype(jnp.bfloat16)]
    add x1 -> x0, other arithmetic: 4.92 us -> none  [on_device(): beta_one * moment_in + (1.0 - beta_one) * gradient.astype(jnp.float32)]
    all_gather x1, waiting for transfers between devices: 81.6 us -> 86.3 us  [on_device(): both = lax.all_gather(both, 'fsdp', axis=0, tiled=True)]
  transfers between devices with their start and end apart: 3 -> 3, of which waited for: 3 -> 2; matrix products, arithmetic and copies ran while one was open for 7% -> 7% of each run, Pallas kernels for 11% -> 16%
where the time goes in v3:
time: 309 us; the launch traced here: 304 us
  Pallas kernels  138 us (45%)
  waiting for transfers between devices  95.1 us (31%)
  matrix products  28.5 us (9%)
  between operations  15 us (5%)
  other arithmetic  11.6 us (4%)
  starting transfers between devices  8.33 us (3%)
  local copies, waits for them, and re-layouts  7.07 us (2%)
    pallas_call x2, Pallas kernels, orthogonal_rows(): pl.pallas_call(functools.partial(kernel, prev, count), out_shape=outs, sc...  117 us
    all_gather x1, waiting for transfers between devices, on_device(): both = lax.all_gather(both, 'fsdp', axis=0, tiled=True)  86.3 us
    dot_general x2, matrix products, mm(): return lax.dot_general(a, b, dims, preferred_element_type=jnp.float32)  28.5 us
    pallas_call x1, Pallas kernels, rotate(): pl.pallas_call(rotate_kernel, grid=(rows // BAND,), in_specs=[pl.BlockSpe...  21.2 us
    all_to_all x1, starting transfers between devices, sum_over_all(): lax.all_to_all(copies, axes, 0, 0, tiled=True)[:, :1]  8.25 us
    all_to_all x1, waiting for transfers between devices, sum_over_all(): lax.all_to_all(copies, axes, 0, 0, tiled=True)[:, :1]  8.09 us
  transfers between devices with their start and end apart: 3, of which 2 were waited for; matrix products, arithmetic and copies ran while one was open for 7% of the time, Pallas kernels for 16%

profile of v3, /device:TPU:0, one launch (start us, length us, event | category | flops | bytes accessed | tf_op | source)
XLA Modules:
  0.0 304.1 jit_solution(16150752960837823587)
XLA Ops:
  7.2 0.0 copy-start
  7.2 0.0 all-gather.4.cloned.1.call-start
  7.2 1.9 slice_bitcast_fusion
  9.2 2.0 pad_maximum_fusion
  11.1 0.0 all-gather.4.cloned.1.call-update
  11.2 0.0 all-gather.6.cloned.1.call-start
  11.2 0.7 all-gather.6.cloned.1.call-update
  11.9 0.0 copy-done
  11.9 5.7 %fusion.15 = (bf16[2048,512]{1,0:T(8,128)(2,1)}, f32[2048,512]{1,0:T(8,128)}) fusion(bf16[2048,512]{1,0:T(8,128)(2,1)S(1)} %copy-done, f32[2048,512]{1,0:T(8,128)} %param.8), kind=kLoop, calls=%fused_computation.13 | loop fusion | flops 5242880 | bytes 12582912 | tf_op jit(solution)/shard_map/convert_element_type | solution.py:236
  17.6 86.3 %all-gather.4.cloned.1.call-done = bf16[2048,3072]{1,0:T(8,128)(2,1)} async-done(((bf16[128,3072]{1,0:T(8,128)(2,1)}), bf16[2048,3072]{1,0:T(8,128)(2,1)}) %all-gather.4.cloned.1.call-update) | async-done | bytes 12582928 | tf_op jit(solution)/shard_map/all_gather | solution.py:232
  103.9 14.2 %fusion.10.refs_0_ = bf16[1024,2048]{1,0:T(8,128)(2,1)} fusion(bf16[2048,3072]{1,0:T(8,128)(2,1)} %all-gather.4.cloned.1.call-done), kind=kOutput, calls=%fused_computation.9 | convolution fusion | flops 8592031744 | bytes 16777216 | tf_op jit(solution)/shard_map/dot_general | solution.py:63
  118.1 47.2 %shard_map.84 = (bf16[1024,2048]{1,0:T(8,128)(2,1)}, bf16[1024,2048]{1,0:T(8,128)(2,1)}) custom-call(bf16[1024,2048]{1,0:T(8,128)(2,1)} %fusion.10.refs_0_), custom_call_target="tpu_custom_call" | custom-call | tf_op jit(solution)/shard_map/pallas_call | solution.py:169
  165.3 0.0 all-gather.6.cloned.1.call-done
  165.3 14.3 %convert_bitcast_fusion.refs_0_ = bf16[1024,2048]{1,0:T(8,128)(2,1)} fusion(bf16[1,2048,1024]{2,1,0:T(8,128)(2,1)} %all-gather.6.cloned.1.call-done, bf16[2048,3072]{1,0:T(8,128)(2,1)} %all-gather.4.cloned.1.call-done), kind=kOutput, calls=%fused_computation.8 | convolution fusion | flops 8592031744 | bytes 16777216 | tf_op jit(solution)/shard_map/dot_general | solution.py:63
  179.6 0.0 copy-start.1
  179.6 70.1 %shard_map.85 = (bf16[2048,2048]{1,0:T(8,128)(2,1)}, f32[2048,128]{1,0:T(8,128)}) custom-call(bf16[1024,2048]{1,0:T(8,128)(2,1)} %convert_bitcast_fusion.refs_0_, bf16[1024,2048]{1,0:T(8,128)(2,1)} %get-tuple-element.11.refs_1_, bf16[1024,2048]{1,0:T(8,128)(2,1)} %get-tuple-element.12.refs_2_), custom_call_target="tpu_custom_call" | custom-call | tf_op jit(solution)/shard_map/pallas_call | solution.py:169
  249.7 0.0 copy-done.1
  249.7 0.0 copy-start.2
  249.7 21.2 %shard_map.86 = (f32[2048,512]{1,0:T(8,128)}, f32[512,2048]{1,0:T(8,128)}, f32[1,2048]{1,0:T(1,128)S(1)}) custom-call(bf16[2048,2048]{1,0:T(8,128)(2,1)} %get-tuple-element.13.q_ref, bf16[2048,512]{1,0:T(8,128)(2,1)S(1)} %copy-done, bf16[2048,512]{1,0:T(8,128)(2,1)S(1)} %copy-done.1, f32[2048,512]{1,0:T(8,128)} %second_ref.1), custom_call_target="tpu_custom_call" | custom-call | tf_op jit(solution)/shard_map/pallas_call | solution.py:207
  270.9 0.6 reduce_sum.18
  271.5 1.3 broadcast_in_dim.4
  272.8 8.3 %all-to-all-start = ((f32[128,1,128]{2,1,0:T(1,128)}), f32[128,1,128]{2,1,0:T(1,128)S(1)}, u32[]{:S(2)}, u32[]{:S(2)}) async-start(f32[128,1,128]{2,1,0:T(1,128)} %broadcast_in_dim.4), calls=%async_computation | async-start | bytes 131072 | tf_op jit(solution)/shard_map/all_to_all | solution.py:225
  281.1 0.0 copy-done.2
  281.1 1.3 copy.18
  282.4 8.1 %all-to-all-done = f32[128,1,128]{2,1,0:T(1,128)S(1)} async-done(((f32[128,1,128]{2,1,0:T(1,128)}), f32[128,1,128]{2,1,0:T(1,128)S(1)}, u32[]{:S(2)}, u32[]{:S(2)}) %all-to-all-start) | async-done | bytes 65568 | tf_op jit(solution)/shard_map/all_to_all | solution.py:225
  290.5 0.6 slice_reduce_fusion
  291.9 2.7 multiply_convert_fusion
  294.5 2.5 copy.17
Async XLA Ops:
  7.2 4.8 %copy-start = (bf16[2048,512]{1,0:T(8,128)(2,1)S(1)}, bf16[2048,512]{1,0:T(8,128)(2,1)}, u32[]{:S(2)}) copy-start(bf16[2048,512]{1,0:T(8,128)(2,1)} %gradient_ref.1) | copy-start | bytes 6291460
  7.2 96.8 %all-gather.4.cloned.1.call-start = ((), (), s32[]{:S(2)}) async-start(), calls=%async_computation.1 | async-start | bytes 13369344 | tf_op jit(solution)/shard_map/all_gather | solution.py:232
  11.2 154.1 %all-gather.6.cloned.1.call-start = ((), (), s32[]{:S(2)}) async-start(), calls=%async_computation.2 | async-start | bytes 4456448 | tf_op jit(solution)/shard_map/all_gather | solution.py:234
  179.6 70.1 %copy-start.1 = (bf16[2048,512]{1,0:T(8,128)(2,1)S(1)}, bf16[2048,512]{1,0:T(8,128)(2,1)}, u32[]{:S(2)}) copy-start(bf16[2048,512]{1,0:T(8,128)(2,1)} %get-tuple-element.30.moment_ref) | copy-start | bytes 6291460
  249.7 31.4 %copy-start.2 = (f32[2048,128]{1,0:T(8,128)S(1)}, f32[2048,128]{1,0:T(8,128)}, u32[]{:S(2)}) copy-start(f32[2048,128]{1,0:T(8,128)} %get-tuple-element.17) | copy-start | bytes 3145732
  272.8 17.7 %all-to-all-start = ((f32[128,1,128]{2,1,0:T(1,128)}), f32[128,1,128]{2,1,0:T(1,128)S(1)}, u32[]{:S(2)}, u32[]{:S(2)}) async-start(f32[128,1,128]{2,1,0:T(1,128)} %broadcast_in_dim.4), calls=%async_computation | async-start | bytes 131072 | tf_op jit(solution)/shard_map/all_to_all | solution.py:225
Sparse Core Ops, SparseCore 0:
  11.3 92.5 all-gather.3
  106.1 51.2 all-gather.5
